TPU v7x, 32 devices: a whole 2x2x4 slice. The times are simulated.
32 devices in a mesh: blk: 16 (over z, y, core), copy: 2 (over x).
Axes of the slice: x: 2, y: 2, z: 4, core: 2. Of those that a mesh axis runs over, the one named last changes fastest.
Arguments:
- features: float32 [4096, 512], P(('blk', 'copy')), may hold values from -16 to 16
- attend_source: float32 [8, 64], replicated, may hold values from -1 to 1
- attend_target: float32 [8, 64], replicated, may hold values from -1 to 1
- key_blocks: int32 [32, 6], P(('blk', 'copy')), may hold values from 0 to 31, as said below
- live_slots: int32 [32], P(('blk', 'copy')), may hold values from 3 to 6, as said below
- edge_bits: int32 [32, 6, 16, 128], P(('blk', 'copy')), may hold values from 0 to 255
- cotangent: float32 [4096, 512], P(('blk', 'copy')), may hold values from -6 to 6
Outputs:
- layer_out: float32 [4096, 512], P(('blk', 'copy'))
- feature_grad: float32 [4096, 512], P(('blk', 'copy'))
- source_grad: float32 [8, 64], replicated
- target_grad: float32 [8, 64], replicated
Inputs may be any that keep to these rules, and one draw needn't show every extreme that they name: `key_blocks`: slot 0 of query block q holds q itself. The other slots hold distinct blocks, each in the panel of q (the 2 blocks b with b // 2 equal to q // 2) or in one of the two panels beside it, panel numbers taken modulo 32 // 2; slot 1 lies in the panel before and slot 2 in the panel after. `live_slots`: some query block uses all 6 slots.
All inputs are finite; a program needn't handle non-finite values.
Results may differ from a plain program's by a relative error of at most 0.0003.
Values sent between devices are 32-bit elements; how exact they have to be, the bound alone decides.
A program may use at most 64 MiB of HBM per device.

v0:
```python
import jax
import jax.numpy as jnp
from jax import lax
from jax.sharding import PartitionSpec as P

precise = lax.Precision.HIGHEST


def shifted(value, axis, steps):
    count = lax.axis_size(axis)
    pairs = [(source, (source + steps) % count) for source in range(count)]
    return lax.ppermute(value, axis, pairs)


def unpack_mask(mask_words):
    bit_shift = jnp.arange(8, dtype=jnp.int32)
    bit_values = jnp.bitwise_and(
        jnp.right_shift(mask_words[:, None, :], bit_shift[None, :, None]), 1
    )
    return bit_values.reshape(mask_words.shape[0] * 8, mask_words.shape[1]) > 0


def head_logits(node_rows, vector):
    head_count, head_width = vector.shape
    shaped = node_rows.reshape(node_rows.shape[0], head_count, head_width)
    return jnp.einsum("khc,hc->hk", shaped, vector, precision=precise)


def add_rows(panel, piece, row_start):
    current = lax.dynamic_slice_in_dim(panel, row_start, piece.shape[0], 0)
    return lax.dynamic_update_slice_in_dim(panel, current + piece, row_start, 0)


def per_device(
    features, attend_source, attend_target, key_blocks, live_slots, edge_bits, cotangent
):
    head_count, head_width = attend_source.shape
    rows_dev, model_width = features.shape
    blocks_dev = key_blocks.shape[0]
    block_rows = rows_dev // blocks_dev
    copies = lax.axis_size("copy")
    cycle_size = lax.axis_size("blk")
    panel_blocks = copies * blocks_dev
    cycle_index = lax.axis_index("blk")
    first_block = (cycle_index * copies + lax.axis_index("copy")) * blocks_dev
    own_panel = lax.all_gather(features, "copy", axis=0, tiled=True)
    prev_panel = shifted(own_panel, "blk", 1)
    next_panel = shifted(own_panel, "blk", -1)
    diagonal = jnp.arange(block_rows)[:, None] == jnp.arange(block_rows)[None, :]

    def slot_scores(block_local, slot_pos, target_query):
        block_id = key_blocks[block_local, slot_pos]
        offset = jnp.mod(block_id // panel_blocks - cycle_index, cycle_size)
        row_start = block_id % panel_blocks * block_rows
        from_prev = lax.dynamic_slice_in_dim(prev_panel, row_start, block_rows, 0)
        from_own = lax.dynamic_slice_in_dim(own_panel, row_start, block_rows, 0)
        from_next = lax.dynamic_slice_in_dim(next_panel, row_start, block_rows, 0)
        key_rows = jnp.where(offset == 0, from_own, jnp.where(offset == 1, from_next, from_prev))
        source_keys = head_logits(key_rows, attend_source)
        logit_sum = target_query[:, None, :] + source_keys[:, :, None]
        leaky_score = jnp.where(logit_sum > 0, logit_sum, 0.2 * logit_sum)
        allowed = unpack_mask(edge_bits[block_local, slot_pos])
        allowed = jnp.logical_or(
            allowed, jnp.logical_and(diagonal, block_id == first_block + block_local)
        )
        value_rows = key_rows.reshape(block_rows, head_count, head_width)
        return (offset, row_start, value_rows, logit_sum, leaky_score, allowed)

    panel_zero = jnp.zeros(own_panel.shape, jnp.float32)
    prev_part, own_part, next_part = (panel_zero, panel_zero, panel_zero)
    source_att = jnp.zeros((head_count, head_width), jnp.float32)
    block_local = 0
    query_values = features.reshape(block_rows, head_count, head_width)
    target_query = head_logits(features, attend_target)
    live_count = live_slots[block_local]

    def forward_step(slot_pos, loop_state, block_local=block_local, target_query=target_query):
        row_peak, row_norm, weighted = loop_state
        _, _, value_rows, _, leaky_score, allowed = slot_scores(block_local, slot_pos, target_query)
        masked = jnp.where(allowed[None], leaky_score, -jnp.inf)
        new_peak = jnp.maximum(row_peak, jnp.max(masked, axis=1))
        factor = jnp.exp(row_peak - new_peak)
        weights = jnp.where(allowed[None], jnp.exp(leaky_score - new_peak[:, None, :]), 0.0)
        row_norm = row_norm * factor + jnp.sum(weights, axis=1)
        weighted = weighted * factor.T[:, :, None] + jnp.einsum(
            "hkq,khc->qhc", weights, value_rows, precision=precise
        )
        return (new_peak, row_norm, weighted)

    start_state = (
        jnp.full((head_count, block_rows), -jnp.inf, jnp.float32),
        jnp.zeros((head_count, block_rows), jnp.float32),
        jnp.zeros((block_rows, head_count, head_width), jnp.float32),
    )
    row_peak, row_norm, weighted = lax.fori_loop(0, live_count, forward_step, start_state)
    agg = weighted / row_norm.T[:, :, None]
    log_total = row_peak + jnp.log(row_norm)
    out_blocks = jax.nn.elu(agg).reshape(block_rows, model_width)
    cot_rows = cotangent.reshape(block_rows, head_count, head_width)
    grad_agg = cot_rows * jnp.where(agg > 0, 1.0, jnp.exp(agg))
    row_delta = jnp.einsum("qhc,qhc->hq", grad_agg, agg, precision=precise)

    def backward_step(
        slot_pos,
        loop_state,
        block_local=block_local,
        target_query=target_query,
        grad_agg=grad_agg,
        row_delta=row_delta,
        log_total=log_total,
    ):
        prev_acc, own_acc, next_acc, target_part, source_acc = loop_state
        offset, row_start, value_rows, logit_sum, leaky_score, allowed = slot_scores(
            block_local, slot_pos, target_query
        )
        weights = jnp.where(allowed[None], jnp.exp(leaky_score - log_total[:, None, :]), 0.0)
        prob_grad = jnp.einsum("qhc,khc->hkq", grad_agg, value_rows, precision=precise)
        score_grad = (
            weights * (prob_grad - row_delta[:, None, :]) * jnp.where(logit_sum > 0, 1.0, 0.2)
        )
        target_part = target_part + jnp.sum(score_grad, axis=1)
        source_part = jnp.sum(score_grad, axis=2)
        value_grad = jnp.einsum("hkq,qhc->khc", weights, grad_agg, precision=precise)
        key_grad = (value_grad + source_part.T[:, :, None] * attend_source[None]).reshape(
            block_rows, model_width
        )
        source_acc = source_acc + jnp.einsum(
            "hk,khc->hc", source_part, value_rows, precision=precise
        )
        prev_acc = add_rows(prev_acc, jnp.where(offset == cycle_size - 1, key_grad, 0.0), row_start)
        own_acc = add_rows(own_acc, jnp.where(offset == 0, key_grad, 0.0), row_start)
        next_acc = add_rows(next_acc, jnp.where(offset == 1, key_grad, 0.0), row_start)
        return (prev_acc, own_acc, next_acc, target_part, source_acc)

    back_state = (
        prev_part,
        own_part,
        next_part,
        jnp.zeros((head_count, block_rows), jnp.float32),
        source_att,
    )
    prev_part, own_part, next_part, target_part, source_att = lax.fori_loop(
        0, live_count, backward_step, back_state
    )
    local_terms = (target_part.T[:, :, None] * attend_target[None]).reshape(block_rows, model_width)
    target_att = jnp.einsum("hq,qhc->hc", target_part, query_values, precision=precise)
    from_next = shifted(prev_part, "blk", -1)
    from_prev = shifted(next_part, "blk", 1)
    panel_total = own_part + from_next + from_prev
    own_grad = lax.psum_scatter(panel_total, "copy", scatter_dimension=0, tiled=True)
    feature_grad = own_grad + local_terms
    source_grad, target_grad = lax.psum((source_att, target_att), ("blk", "copy"))
    return (out_blocks, feature_grad, source_grad, target_grad)


def solution(mesh):
    placed = (
        P(("blk", "copy"), None),
        P(),
        P(),
        P(("blk", "copy"), None),
        P(("blk", "copy")),
        P(("blk", "copy"), None, None, None),
        P(("blk", "copy"), None),
    )
    return jax.shard_map(
        per_device,
        mesh=mesh,
        in_specs=placed,
        out_specs=(P(("blk", "copy"), None), P(("blk", "copy"), None), P(), P()),
        check_vma=False,
    )
```

profile of v0, /device:TPU:1, one launch (start us, length us, event | category | flops | bytes accessed | tf_op | source)
XLA Modules:
  0.0 201.3 jit_solution(13442062027237379613)
XLA Ops:
  7.2 1.1 copy.18
  8.3 8.9 %all_gather.3 = f32[256,512]{0,1:T(8,128)S(1)} all-gather(f32[128,512]{0,1:T(8,128)S(1)} %copy.18), channel_id=1, replica_groups=mesh['blk'=16,'copy'=2] {'copy'}, dimensions={0}, use_global_device_ids=true | all-gather | bytes 786432 | tf_op jit(solution)/shard_map/all_gather | solution.py:46
  17.2 2.6 %collective-permute-start.1 = (f32[256,512]{0,1:T(8,128)S(1)}, f32[256,512]{0,1:T(8,128)S(1)}, u32[]{:S(2)}, u32[]{:S(2)}) collective-permute-start(f32[256,512]{0,1:T(8,128)S(1)} %all_gather.3), channel_id=1, source_target_pairs={{0,2},{2,4},{4,6},{6,8},{8,10},{10,12},{12,14},{14,16},{16,18},{18... | collective-permute-start | bytes 1572872 | tf_op jit(solution)/shard_map/ppermute | solution.py:12
  19.8 0.1 copy.20
  19.9 0.7 copy-done.4
  20.6 0.3 fusion.46
  20.9 10.6 %collective-permute-done.1 = f32[256,512]{0,1:T(8,128)S(1)} collective-permute-done((f32[256,512]{0,1:T(8,128)S(1)}, f32[256,512]{0,1:T(8,128)S(1)}, u32[]{:S(2)}, u32[]{:S(2)}) %collective-permute-start.1) | collective-permute-done | bytes 524320 | tf_op jit(solution)/shard_map/ppermute | solution.py:12
  31.5 2.5 %collective-permute-done = f32[256,512]{0,1:T(8,128)S(1)} collective-permute-done((f32[256,512]{0,1:T(8,128)S(1)}, f32[256,512]{0,1:T(8,128)S(1)}, u32[]{:S(2)}, u32[]{:S(2)}) %collective-permute-start) | collective-permute-done | bytes 524320 | tf_op jit(solution)/shard_map/ppermute | solution.py:12
  34.0 0.7 copy-done.1
  34.7 22.2 %while.40 = (s32[]{:T(128)}, f32[8,128]{1,0:T(8,128)S(1)}, f32[8,128]{1,0:T(8,128)S(1)}, f32[128,8,64]{0,2,1:T(8,128)S(1)}, s32[]{:T(128)}, /*index=5*/s32[1,6,1...) while((s32[]{:T(128)}, f32[8,128]{1,0:T(8,128)S(1)}, ...), condition=%wide.region_3.4_spmd.clone, body=%wide.region_0.3_spmd.clone.sunk | while | flops 104303656 | bytes 2286219 | solution.py:95
  35.4 0.6 constant_dynamic-slice_fusion.4
  39.2 0.7 dynamic-slice_bitcast_fusion.4
  40.2 0.3 fusion.84
  40.5 0.2 select_reduce_fusion.2
  40.8 0.8 fusion.88
  41.6 0.2 fusion.87
  42.5 0.6 constant_dynamic-slice_fusion.4
  46.4 0.7 dynamic-slice_bitcast_fusion.4
  47.4 0.3 fusion.84
  47.7 0.2 select_reduce_fusion.2
  48.0 0.8 fusion.88
  48.8 0.2 fusion.87
  49.7 0.6 constant_dynamic-slice_fusion.4
  53.6 0.7 dynamic-slice_bitcast_fusion.4
  54.6 0.3 fusion.84
  54.9 0.2 select_reduce_fusion.2
  55.1 0.8 fusion.88
  55.9 0.2 fusion.87
  56.9 0.9 fusion.40
  58.1 29.9 %while.41 = (s32[]{:T(128)}, f32[256,512]{0,1:T(8,128)S(1)}, f32[256,512]{0,1:T(8,128)S(1)}, f32[256,512]{0,1:T(8,128)S(1)}, f32[8,128]{1,0:T(8,128)S(1)}, /*ind...) while((s32[]{:T(128)}, f32[256,512]{0,1:T(8,128)S(1)}, ...), condition=%wide.region_7.8_spmd.clone, body=%wide.region_4.7_spmd.clone.sunk | while | flops 206011936 | bytes 6703843 | solution.py:142
  58.7 0.6 constant_dynamic-slice_fusion.5
  62.6 0.7 dynamic-slice_bitcast_fusion.5
  63.6 0.3 fusion.96
  63.9 0.6 copy-done.3
  64.5 1.3 fusion.98
  65.8 0.5 fusion.99
  66.3 1.3 broadcast_select_fusion.4
  67.7 0.1 constant_dynamic-update-slice_fusion.5
  68.5 0.6 constant_dynamic-slice_fusion.5
  72.4 0.7 dynamic-slice_bitcast_fusion.5
  73.3 0.3 fusion.96
  73.7 0.6 copy-done.3
  74.3 1.3 fusion.98
  75.6 0.5 fusion.99
  76.1 1.3 broadcast_select_fusion.4
  77.5 0.1 constant_dynamic-update-slice_fusion.5
  78.2 0.6 constant_dynamic-slice_fusion.5
  82.1 0.7 dynamic-slice_bitcast_fusion.5
  83.1 0.3 fusion.96
  83.4 0.6 copy-done.3
  84.0 1.3 fusion.98
  85.3 0.5 fusion.99
  85.8 1.3 broadcast_select_fusion.4
  87.2 0.1 constant_dynamic-update-slice_fusion.5
  88.0 46.5 %collective-permute-start.2 = (f32[256,512]{0,1:T(8,128)S(1)}, f32[256,512]{0,1:T(8,128)S(1)}, u32[]{:S(2)}, u32[]{:S(2)}) collective-permute-start(f32[256,512]{0,1:T(8,128)S(1)} %get-tuple-element.558), channel_id=1, source_target_pairs={{0,30},{2,0},{4,2},{6,4},{8,6},{10,8},{12,10},{14,12},{16,14},{18,... | collective-permute-start | bytes 1572872 | tf_op jit(solution)/shard_map/ppermute | solution.py:12
  134.5 1.5 collective-permute-done.2
  136.1 4.6 %collective-permute-done.3 = f32[256,512]{0,1:T(8,128)S(1)} collective-permute-done((f32[256,512]{0,1:T(8,128)S(1)}, f32[256,512]{0,1:T(8,128)S(1)}, u32[]{:S(2)}, u32[]{:S(2)}) %collective-permute-start.3) | collective-permute-done | bytes 524320 | tf_op jit(solution)/shard_map/ppermute | solution.py:12
  140.7 0.9 add_add_fusion
  141.7 0.8 copy-done
  142.5 0.8 copy.21
  143.4 0.5 fusion.47
  143.9 48.7 %all-reduce = (f32[8,64]{1,0:T(8,128)}, f32[8,64]{1,0:T(8,128)}) all-reduce(f32[8,64]{1,0:T(8,128)S(1)} %get-tuple-element.561, f32[8,64]{1,0:T(8,128)S(1)} %bitcast.174), channel_id=1, replica_groups=mesh['blk'=16,'copy'=2] {'blk','copy'}, use_global_device_ids=true, to_apply=%region_9.10 | all-reduce | flops 1024 | bytes 8192 | tf_op jit(solution)/shard_map/psum | solution.py:152
  192.6 1.1 fusion.41
  193.6 0.8 copy.22
  (68 shorter events, 2.1 us)
Async XLA Ops:
  7.2 185.4 %reduce-scatter.2.cloned.1.call-start = ((), (), s32[]{:S(2)}) async-start(), calls=%async_computation.1 | async-start | bytes 786432 | tf_op jit(solution)/shard_map/reduce_scatter | solution.py:150
  8.3 11.5 %copy-start.2 = (f32[128,512]{1,0:T(8,128)S(1)}, f32[128,512]{1,0:T(8,128)}, u32[]{:S(2)}) copy-start(f32[128,512]{1,0:T(8,128)} %param.17) | copy-start | bytes 786436
  17.2 14.4 %collective-permute-start.1 = (f32[256,512]{0,1:T(8,128)S(1)}, f32[256,512]{0,1:T(8,128)S(1)}, u32[]{:S(2)}, u32[]{:S(2)}) collective-permute-start(f32[256,512]{0,1:T(8,128)S(1)} %all_gather.3), channel_id=1, source_target_pairs={{0,2},{2,4},{4,6},{6,8},{8,10},{10,12},{12,14},{14,16},{16,18},{18... | collective-permute-start | bytes 1572872 | tf_op jit(solution)/shard_map/ppermute | solution.py:12
  19.8 14.2 %collective-permute-start = (f32[256,512]{0,1:T(8,128)S(1)}, f32[256,512]{0,1:T(8,128)S(1)}, u32[]{:S(2)}, u32[]{:S(2)}) collective-permute-start(f32[256,512]{0,1:T(8,128)S(1)} %all_gather.3), channel_id=1, source_target_pairs={{0,30},{2,0},{4,2},{6,4},{8,6},{10,8},{12,10},{14,12},{16,14},{18,... | collective-permute-start | bytes 1572872 | tf_op jit(solution)/shard_map/ppermute | solution.py:12
  19.9 0.7 copy-start.4
  34.0 0.7 copy-start.1
  34.0 0.7 copy-start.5
  63.6 1.0 copy-start.3
  73.3 1.0 copy-start.3
  83.1 1.0 copy-start.3
  88.0 48.1 %collective-permute-start.2 = (f32[256,512]{0,1:T(8,128)S(1)}, f32[256,512]{0,1:T(8,128)S(1)}, u32[]{:S(2)}, u32[]{:S(2)}) collective-permute-start(f32[256,512]{0,1:T(8,128)S(1)} %get-tuple-element.558), channel_id=1, source_target_pairs={{0,30},{2,0},{4,2},{6,4},{8,6},{10,8},{12,10},{14,12},{16,14},{18,... | collective-permute-start | bytes 1572872 | tf_op jit(solution)/shard_map/ppermute | solution.py:12
  134.5 6.1 %collective-permute-start.3 = (f32[256,512]{0,1:T(8,128)S(1)}, f32[256,512]{0,1:T(8,128)S(1)}, u32[]{:S(2)}, u32[]{:S(2)}) collective-permute-start(f32[256,512]{0,1:T(8,128)S(1)} %get-tuple-element.559), channel_id=1, source_target_pairs={{0,2},{2,4},{4,6},{6,8},{8,10},{10,12},{12,14},{14,16},{16,18},{18... | collective-permute-start | bytes 1572872 | tf_op jit(solution)/shard_map/ppermute | solution.py:12
  141.6 0.9 copy-start
Sparse Core Ops, SparseCore 0:
  141.7 23.8 reduce-scatter.1
where the time goes:
time: 202 us; the launch traced here: 201 us
  blocking collectives  57.6 us (29%)
  starting transfers between devices  49.2 us (24%)
  loops' own time  25.3 us (13%)
  waiting for transfers between devices  19.2 us (10%)
  local copies, waits for them, and re-layouts  15.4 us (8%)
  matrix products  14.5 us (7%)
  between operations  14.2 us (7%)
  other arithmetic  5.94 us (3%)
    ppermute x4, starting transfers between devices, shifted(): return lax.ppermute(value, axis, pairs)  49.2 us
    psum x1, blocking collectives, per_device(): lax.psum((source_att, target_att), ('blk', 'copy'))  48.7 us
    ppermute x4, waiting for transfers between devices, shifted(): return lax.ppermute(value, axis, pairs)  19.2 us
    another operation x1, loops' own time, per_device(): lax.fori_loop(0, live_count, forward_step, start_state)  12.7 us
    another operation x1, loops' own time, per_device(): lax.fori_loop(0, live_count, backward_step, back_state)  12.7 us
    all_gather x1, blocking collectives, per_device(): own_panel = lax.all_gather(features, 'copy', axis=0, tiled=True)  8.87 us
    unnamed x14, local copies, waits for them, and re-layouts  5.06 us
    shift_right_arithmetic x18, local copies, waits for them, and re-layouts, unpack_mask(): jnp.right_shift(mask_words[:, None, :], bit_shift[None, :, None])  4.76 us
  transfers between devices with their start and end apart: 5, of which 4 were waited for; matrix products, arithmetic and copies ran while one was open for 1% of the time, Pallas kernels for 0%

commit v1 on v0

v1 whole, which is shorter than its diff:
```python
import functools

import jax
import jax.numpy as jnp
from jax import lax
from jax.experimental import pallas as pl
from jax.experimental.pallas import tpu as pltpu
from jax.sharding import PartitionSpec as P

precise = lax.Precision.HIGHEST
MESH = pl.DeviceIdType.MESH
f32 = jnp.float32
bf16 = jnp.bfloat16


def split(value):
    high = value.astype(bf16)
    return high, (value - high.astype(f32)).astype(bf16)


def mm(left, right):
    return jnp.dot(left, right, preferred_element_type=f32)


def kernel(
    cycle,
    copies,
    feat_ref,
    source_ref,
    target_ref,
    blocks_ref,
    live_ref,
    edges_ref,
    cot_ref,
    out_ref,
    grad_ref,
    sgrad_ref,
    tgrad_ref,
    feats,
    srcs,
    bits,
    w_hi,
    w_lo,
    w_slope,
    agg,
    probs_a,
    probs_b,
    vals_hi,
    vals_lo,
    delta_s,
    sent,
    got,
    dst_sum,
    src_att,
    red,
    red2,
    feat_send,
    feat_recv,
    src_send,
    src_recv,
    grad_send,
    grad_recv,
    red_send,
    red_recv,
    red2_send,
    red2_recv,
):
    rows, width = feat_ref.shape
    heads, head = source_ref.shape
    slots = edges_ref.shape[0]
    count = 3 * copies
    pairs = heads // 2
    blk = lax.axis_index("blk")
    cp = lax.axis_index("copy")

    def place(c):
        group, turn = c // copies, c % copies
        shift = (group + 1) % 3 - 1
        return lax.rem(blk + shift + cycle, cycle), lax.rem(cp + turn, copies)

    def mirror(c):
        group, turn = c // copies, c % copies
        return (3 - group) % 3 * copies + (copies - turn) % copies

    barrier = pltpu.get_barrier_semaphore()
    for c in range(1, count):
        pl.semaphore_signal(barrier, inc=1, device_id=place(c), device_id_type=MESH)

    def greet(step, carry):
        pl.semaphore_signal(
            barrier, inc=1, device_id=(lax.rem(blk + step, cycle), cp), device_id_type=MESH
        )
        return carry

    lax.fori_loop(2, cycle - 1, greet, 0)

    lane = lax.broadcasted_iota(jnp.int32, (heads, width), 1)
    head_row = lax.broadcasted_iota(jnp.int32, (heads, width), 0)
    on_head = lane // head == head_row
    wide_source = jnp.where(on_head, jnp.concatenate([source_ref[...]] * heads, 1), 0.0)
    wide_target = jnp.where(on_head, jnp.concatenate([target_ref[...]] * heads, 1), 0.0)
    logits = lax.dot_general(
        jnp.concatenate([wide_source, wide_target], 0),
        feat_ref[...],
        (((1,), (1,)), ((), ())),
        precision=precise,
        preferred_element_type=f32,
    )
    srcs[0] = logits[:heads]
    dst = logits[heads:]

    pl.semaphore_wait(barrier, count - 1 + cycle - 3)

    def src_copy(c):
        return pltpu.make_async_remote_copy(
            src_ref=srcs.at[0],
            dst_ref=srcs.at[mirror(c)],
            send_sem=src_send.at[c],
            recv_sem=src_recv.at[mirror(c)],
            device_id=place(c),
            device_id_type=MESH,
        )

    def feat_copy(c):
        return pltpu.make_async_remote_copy(
            src_ref=feat_ref,
            dst_ref=feats.at[mirror(c)],
            send_sem=feat_send.at[c],
            recv_sem=feat_recv.at[mirror(c)],
            device_id=place(c),
            device_id_type=MESH,
        )

    def grad_copy(c):
        return pltpu.make_async_remote_copy(
            src_ref=sent.at[c],
            dst_ref=got.at[mirror(c)],
            send_sem=grad_send.at[c],
            recv_sem=grad_recv.at[mirror(c)],
            device_id=place(c),
            device_id_type=MESH,
        )

    for c in range(1, count):
        src_copy(c).start()
    for c in range(1, count):
        feat_copy(c).start()
    feats[0] = feat_ref[...]

    live = live_ref[0]
    for c in range(count):
        there, turn = place(c)
        block = there * copies + turn
        words = jnp.zeros(bits.shape[1:], jnp.int32)
        for slot in range(slots):
            chosen = jnp.logical_and(blocks_ref[0, slot] == block, slot < live)
            words = words + edges_ref[slot] * jnp.where(chosen, 1, 0)
        bits[c] = words

    cot_t = cot_ref[...].T
    bit = lax.broadcasted_iota(jnp.int32, (rows // 8, 8, rows), 1)
    key_row = lax.broadcasted_iota(jnp.int32, (rows, rows), 0)
    query_lane = lax.broadcasted_iota(jnp.int32, (rows, rows), 1)

    def mask_of(c):
        words = jnp.broadcast_to(bits[c][:, None, :], (rows // 8, 8, rows))
        mask = jnp.bitwise_and(jnp.right_shift(words, bit), 1).reshape(rows, rows)
        self_edge = jnp.where(key_row == query_lane, jnp.where(c == 0, 1, 0), 0)
        return jnp.bitwise_or(mask, self_edge) > 0

    for c in range(1, count):
        src_copy(mirror(c)).wait_recv()

    def peak_step(c, peaks):
        mask = mask_of(c)
        columns = srcs[c].T
        found = []
        for h in range(heads):
            masked = jnp.where(mask, columns[:, h : h + 1], -jnp.inf)
            found.append(jnp.maximum(peaks[h], jnp.max(masked, axis=0, keepdims=True)))
        return tuple(found)

    start = tuple(jnp.full((1, rows), -jnp.inf, f32) for _ in range(heads))
    tops = lax.fori_loop(0, count, peak_step, start)
    dsts = [dst[h : h + 1] for h in range(heads)]
    peaks = []
    for h in range(heads):
        top = dsts[h] + tops[h]
        peaks.append(jnp.where(top > 0, top, 0.2 * top))

    def weight_step(c, norms):
        mask = mask_of(c)
        columns = srcs[c].T
        sums = []
        for h in range(heads):
            logit = dsts[h] + columns[:, h : h + 1]
            up = logit > 0
            score = jnp.where(up, logit, 0.2 * logit)
            weight = jnp.where(mask, jnp.exp(score - peaks[h]), 0.0)
            sums.append(norms[h] + jnp.sum(weight, axis=0, keepdims=True))
            high, low = split(weight)
            w_hi[c, h] = high
            w_lo[c, h] = low
            w_slope[c, h] = jnp.where(up, weight, 0.2 * weight)
        return tuple(sums)

    zero_row = jnp.zeros((1, rows), f32)
    norms = lax.fori_loop(0, count, weight_step, (zero_row,) * heads)

    agg[...] = jnp.zeros(agg.shape, f32)

    def forward_step(c, carry):
        @pl.when(c > 0)
        def _():
            feat_copy(mirror(c)).wait_recv()

        high, low = split(feats[c].T)
        both = jnp.concatenate([high, low], 1)
        for h in range(heads):
            part = pl.ds(h * head, head)
            w_h = w_hi[c, h]
            agg[part, :] += mm(both[h * head : (h + 1) * head], jnp.concatenate([w_h, w_h], 0)) + mm(
                high[h * head : (h + 1) * head], w_lo[c, h]
            )
        return carry

    lax.fori_loop(0, count, forward_step, 0)

    flat_source = jnp.sum(wide_source, axis=0, keepdims=True)
    left = lax.broadcasted_iota(jnp.int32, (rows, rows), 1) < head
    zero_half = jnp.zeros((head, rows), f32)
    zero_tile = jnp.zeros((rows, rows), f32)
    ones_tile = jnp.ones((rows, rows), f32)
    for p in range(pairs):
        scaled, outs = [], []
        for h in (2 * p, 2 * p + 1):
            inverse = 1.0 / norms[h]
            agg_t = agg[h * head : (h + 1) * head, :] * inverse
            raised = jnp.exp(jnp.minimum(agg_t, 0.0))
            outs.append(jnp.where(agg_t > 0, agg_t, raised - 1.0))
            g_t = cot_t[h * head : (h + 1) * head] * jnp.where(agg_t > 0, 1.0, raised)
            delta_s[h] = jnp.sum(g_t * agg_t, axis=0, keepdims=True) * inverse
            scaled.append(g_t * inverse)
        out_ref[:, p * 2 * head : (p + 1) * 2 * head] = jnp.concatenate(outs, 0).T
        g_pair = jnp.concatenate(scaled, 0).T
        block = jnp.concatenate(
            [
                jnp.concatenate([scaled[0], zero_half], 1),
                jnp.concatenate([zero_half, scaled[1]], 1),
            ],
            0,
        )
        high, low = split(block)
        probs_a[p] = jnp.concatenate([high, high], 0)
        probs_b[p] = low
        a_pair = jnp.broadcast_to(flat_source[:, p * 2 * head : (p + 1) * 2 * head], (rows, rows))
        mixed = jnp.concatenate(
            [
                jnp.concatenate([jnp.where(left, g_pair, 0.0), zero_tile], 1),
                jnp.concatenate(
                    [jnp.where(left, a_pair, 0.0), jnp.where(left, ones_tile, 0.0)], 1
                ),
                jnp.concatenate([jnp.where(left, 0.0, g_pair), zero_tile], 1),
                jnp.concatenate(
                    [jnp.where(left, 0.0, a_pair), jnp.where(left, 0.0, ones_tile)], 1
                ),
            ],
            0,
        )
        high, low = split(mixed)
        vals_hi[p] = high
        vals_lo[p] = low

    dst_sum[...] = jnp.zeros(dst_sum.shape, f32)
    src_att[...] = jnp.zeros(src_att.shape, f32)

    def backward_step(step, carry):
        c = lax.rem(step + 1, count)
        for p in range(pairs):
            tile = pl.ds(p * 2 * head, 2 * head)
            value = feats[c, :, tile]
            high, low = split(value)
            prob = mm(jnp.concatenate([high, low], 1), probs_a[p]) + mm(high, probs_b[p])
            highs, lows = [], []
            for side in range(2):
                h = 2 * p + side
                score = w_slope[c, h] * (prob[:, side * rows : (side + 1) * rows] - delta_s[h])
                dst_sum[h] += jnp.sum(score, axis=0, keepdims=True)
                s_hi, s_lo = split(score)
                highs += [w_hi[c, h], s_hi]
                lows += [w_lo[c, h], s_lo]
            left_hi = jnp.concatenate(highs, 1)
            left_lo = jnp.concatenate(lows, 1)
            both = mm(left_hi, vals_hi[p]) + mm(left_lo, vals_hi[p]) + mm(left_hi, vals_lo[p])
            sent[c, :, tile] = both[:, : 2 * head]
            src_att[p] += jnp.sum(both[:, 2 * head :] * value, axis=0, keepdims=True)

        @pl.when(c > 0)
        def _():
            grad_copy(c).start()

        return carry

    lax.fori_loop(0, count, backward_step, 0)

    dst_rows = jnp.concatenate([dst_sum[h] for h in range(heads)], 0)
    tgt_att = jnp.dot(dst_rows, feat_ref[...], precision=precise, preferred_element_type=f32)
    tgt_att = jnp.sum(jnp.where(on_head, tgt_att, 0.0), axis=0, keepdims=True)
    for p in range(pairs):
        red[blk, p : p + 1, :] = src_att[p]
        red[blk, pairs + p : pairs + p + 1, :] = tgt_att[:, p * 2 * head : (p + 1) * 2 * head]

    def red_copy(step, here):
        return pltpu.make_async_remote_copy(
            src_ref=red.at[here],
            dst_ref=red.at[here],
            send_sem=red_send.at[step],
            recv_sem=red_recv.at[here],
            device_id=(lax.rem(blk + step, cycle), cp),
            device_id_type=MESH,
        )

    def red_start(step, carry):
        red_copy(step, blk).start()
        return carry

    lax.fori_loop(1, cycle, red_start, 0)

    own_term = jnp.dot(dst_rows.T, wide_target, precision=precise, preferred_element_type=f32)
    grad_ref[...] = sent[0] + own_term

    def red_wait(step, carry):
        red_copy(step, lax.rem(blk + step, cycle)).wait_recv()
        return carry

    lax.fori_loop(1, cycle, red_wait, 0)
    total = red[0]
    for i in range(1, cycle):
        total = total + red[i]
    red2[cp] = total

    def red2_copy(turn, here):
        return pltpu.make_async_remote_copy(
            src_ref=red2.at[here],
            dst_ref=red2.at[here],
            send_sem=red2_send.at[turn],
            recv_sem=red2_recv.at[here],
            device_id=(blk, lax.rem(cp + turn, copies)),
            device_id_type=MESH,
        )

    for turn in range(1, copies):
        red2_copy(turn, cp).start()

    def grad_step(c, carry):
        grad_copy(mirror(c)).wait_recv()
        grad_ref[...] += got[c]
        return carry

    lax.fori_loop(1, count, grad_step, 0)

    for turn in range(1, copies):
        red2_copy(turn, lax.rem(cp + turn, copies)).wait_recv()
    total = red2[0]
    for i in range(1, copies):
        total = total + red2[i]
    for p in range(pairs):
        for side in range(2):
            h = 2 * p + side
            span = slice(side * head, (side + 1) * head)
            sgrad_ref[h : h + 1, :] = total[p : p + 1, span]
            tgrad_ref[h : h + 1, :] = total[pairs + p : pairs + p + 1, span]

    for c in range(1, count):
        src_copy(c).wait_send()
        feat_copy(c).wait_send()
        grad_copy(c).wait_send()

    def red_sent(step, carry):
        red_copy(step, blk).wait_send()
        return carry

    lax.fori_loop(1, cycle, red_sent, 0)
    for turn in range(1, copies):
        red2_copy(turn, cp).wait_send()


def per_device(
    features, attend_source, attend_target, key_blocks, live_slots, edge_bits, cotangent
):
    heads, head = attend_source.shape
    rows, width = features.shape
    copies = lax.axis_size("copy")
    cycle = lax.axis_size("blk")
    count = 3 * copies
    pairs = heads // 2
    slots, word_rows = edge_bits.shape[1:3]
    vmem = pl.BlockSpec(memory_space=pltpu.VMEM)
    smem = pl.BlockSpec(memory_space=pltpu.SMEM)
    dma = pltpu.SemaphoreType.DMA
    return pl.pallas_call(
        functools.partial(kernel, cycle, copies),
        out_shape=(
            jax.ShapeDtypeStruct((rows, width), f32),
            jax.ShapeDtypeStruct((rows, width), f32),
            jax.ShapeDtypeStruct((heads, head), f32),
            jax.ShapeDtypeStruct((heads, head), f32),
        ),
        in_specs=[vmem, vmem, vmem, smem, smem, vmem, vmem],
        out_specs=(vmem,) * 4,
        scratch_shapes=[
            pltpu.VMEM((count, rows, width), f32),
            pltpu.VMEM((count, heads, rows), f32),
            pltpu.VMEM((count, word_rows, rows), jnp.int32),
            pltpu.VMEM((count, heads, rows, rows), bf16),
            pltpu.VMEM((count, heads, rows, rows), bf16),
            pltpu.VMEM((count, heads, rows, rows), f32),
            pltpu.VMEM((width, rows), f32),
            pltpu.VMEM((pairs, 2 * rows, 2 * rows), bf16),
            pltpu.VMEM((pairs, rows, 2 * rows), bf16),
            pltpu.VMEM((pairs, 4 * rows, 2 * rows), bf16),
            pltpu.VMEM((pairs, 4 * rows, 2 * rows), bf16),
            pltpu.VMEM((heads, 1, rows), f32),
            pltpu.VMEM((count, rows, width), f32),
            pltpu.VMEM((count, rows, width), f32),
            pltpu.VMEM((heads, 1, rows), f32),
            pltpu.VMEM((pairs, 1, 2 * head), f32),
            pltpu.VMEM((cycle, heads, 2 * head), f32),
            pltpu.VMEM((copies, heads, 2 * head), f32),
            dma((count,)),
            dma((count,)),
            dma((count,)),
            dma((count,)),
            dma((count,)),
            dma((count,)),
            dma((cycle,)),
            dma((cycle,)),
            dma((copies,)),
            dma((copies,)),
        ],
        compiler_params=pltpu.CompilerParams(
            collective_id=0, has_side_effects=True, vmem_limit_bytes=52 * 1024 * 1024
        ),
    )(
        features,
        attend_source,
        attend_target,
        key_blocks,
        live_slots,
        edge_bits.reshape(slots, word_rows, rows),
        cotangent,
    )


def solution(mesh):
    placed = (
        P(("blk", "copy"), None),
        P(),
        P(),
        P(("blk", "copy"), None),
        P(("blk", "copy")),
        P(("blk", "copy"), None, None, None),
        P(("blk", "copy"), None),
    )
    return jax.shard_map(
        per_device,
        mesh=mesh,
        in_specs=placed,
        out_specs=(P(("blk", "copy"), None), P(("blk", "copy"), None), P(), P()),
        check_vma=False,
    )
```

time: 202 us -> 57.5 us (0.28)
  blocking collectives: 57.6 us -> 0 us
  starting transfers between devices: 49.2 us -> 0 us
  Pallas kernels: 0 us -> 48.1 us
  loops' own time: 25.3 us -> 0 us
  waiting for transfers between devices: 19.2 us -> 0 us
  matrix products: 14.5 us -> 0 us
  between operations: 14.2 us -> 1.3 us
  local copies, waits for them, and re-layouts: 15.4 us -> 7.31 us
  other arithmetic: 5.94 us -> 0 us
    ppermute x4 -> x0, starting transfers between devices: 49.2 us -> none  [shifted(): return lax.ppermute(value, axis, pairs)]
    psum x1 -> x0, blocking collectives: 48.7 us -> none  [per_device(): lax.psum((source_att, target_att), ('blk', 'copy'))]
    pallas_call x0 -> x1, Pallas kernels: none -> 48.1 us  [per_device(): pl.pallas_call(functools.partial(kernel, cycle, copies), out_shape=(jax.S...]
    another operation x2 -> x0, loops' own time: 25.3 us -> none  [the longest x1 12.7 us: per_device(): lax.fori_loop(0, live_count, forward_step, start_state)]
    ppermute x4 -> x0, waiting for transfers between devices: 19.2 us -> none  [shifted(): return lax.ppermute(value, axis, pairs)]
    dot_general x20 -> x0, matrix products: 14.5 us -> none  [the longest x3 3.89 us: backward_step(): jnp.einsum('qhc,khc->hkq', grad_agg, value_rows, precision=precise)]
    all_gather x1 -> x0, blocking collectives: 8.87 us -> none  [per_device(): own_panel = lax.all_gather(features, 'copy', axis=0, tiled=True)]
    shift_right_arithmetic x18 -> x0, local copies, waits for them, and re-layouts: 4.76 us -> none  [unpack_mask(): jnp.right_shift(mask_words[:, None, :], bit_shift[None, :, None])]
  transfers between devices with their start and end apart: 5 -> 0, of which waited for: 4 -> 0; matrix products, arithmetic and copies ran while one was open for 1% -> 0% of each run, Pallas kernels for 0% -> 0%
where the time goes in v1:
time: 57.5 us; the launch traced here: 56.7 us
  Pallas kernels  48.1 us (84%)
  local copies, waits for them, and re-layouts  7.31 us (13%)
  between operations  1.3 us (2%)
    pallas_call x1, Pallas kernels, per_device(): pl.pallas_call(functools.partial(kernel, cycle, copies), out_shape=(jax.S...  48.1 us
    unnamed x16, local copies, waits for them, and re-layouts  7.31 us

profile of v1, /device:TPU:1, one launch (start us, length us, event | category | flops | bytes accessed | tf_op | source)
XLA Modules:
  0.0 56.7 jit_solution(13518144717236767306)
XLA Ops:
  1.3 0.0 copy-start.5
  1.3 0.6 %copy-done.5 = s32[1,6]{1,0:T(1,128)S(1)} copy-done((s32[1,6]{1,0:T(1,128)S(1)}, s32[1,6]{1,0:T(1,128)}, u32[]{:S(2)}) %copy-start.5) | copy-done | bytes 48
  1.9 0.0 copy-start
  1.9 0.9 %copy-done = f32[128,512]{1,0:T(8,128)S(1)} copy-done((f32[128,512]{1,0:T(8,128)S(1)}, f32[128,512]{1,0:T(8,128)}, u32[]{:S(2)}) %copy-start) | copy-done | bytes 262168
  2.9 0.0 copy-start.1
  2.9 0.9 %copy-done.1 = f32[128,512]{1,0:T(8,128)S(1)} copy-done((f32[128,512]{1,0:T(8,128)S(1)}, f32[128,512]{1,0:T(8,128)}, u32[]{:S(2)}) %copy-start.1) | copy-done | bytes 262168
  3.8 0.0 copy-start.2
  3.8 0.8 %copy-done.2 = s32[1,6,16,128]{3,2,1,0:T(8,128)S(1)} copy-done((s32[1,6,16,128]{3,2,1,0:T(8,128)S(1)}, s32[1,6,16,128]{3,2,1,0:T(8,128)}, u32[]{:S(2)}) %copy-start.2) | copy-done | bytes 49176
  4.6 0.0 copy-start.3
  4.6 0.7 %copy-done.3 = f32[8,64]{1,0:T(8,128)S(1)} copy-done((f32[8,64]{1,0:T(8,128)S(1)}, f32[8,64]{1,0:T(8,128)}, u32[]{:S(2)}) %copy-start.3) | copy-done | bytes 2072
  5.3 0.0 copy-start.4
  5.3 0.7 %copy-done.4 = f32[8,64]{1,0:T(8,128)S(1)} copy-done((f32[8,64]{1,0:T(8,128)S(1)}, f32[8,64]{1,0:T(8,128)}, u32[]{:S(2)}) %copy-start.4) | copy-done | bytes 2072
  6.0 48.1 %shard_map.102 = (f32[128,512]{1,0:T(8,128)S(1)}, f32[128,512]{1,0:T(8,128)S(1)}, f32[8,64]{1,0:T(8,128)S(1)}, f32[8,64]{1,0:T(8,128)S(1)}) custom-call(f32[128,512]{1,0:T(8,128)S(1)} %copy-done, f32[8,64]{1,0:T(8,128)S(1)} %copy-done.3, f32[8,64]{1,0:T(8,128)S(1)} %copy-done.4, s32[1,6]{1,0:T(1,128)S(1)} %copy-done.5, s32[1]{0:T(128)S(6)} %copy.15.live_ref, ...), custom_call_target="tpu_custom_call" | custom-call | tf_op jit(solution)/shard_map/pallas_call | solution.py:401
  54.1 0.7 %copy.16 = f32[128,512]{1,0:T(8,128)} copy(f32[128,512]{1,0:T(8,128)S(1)} %get-tuple-element.8) | data formatting | bytes 524288
  54.8 0.7 %copy.17 = f32[128,512]{1,0:T(8,128)} copy(f32[128,512]{1,0:T(8,128)S(1)} %get-tuple-element.9) | data formatting | bytes 524288
  55.5 0.6 %copy.18 = f32[8,64]{1,0:T(8,128)} copy(f32[8,64]{1,0:T(8,128)S(1)} %get-tuple-element.10) | data formatting | bytes 4096
  56.1 0.6 %copy.19 = f32[8,64]{1,0:T(8,128)} copy(f32[8,64]{1,0:T(8,128)S(1)} %get-tuple-element.11) | data formatting | bytes 4096
Async XLA Ops:
  1.3 0.7 %copy-start.5 = (s32[1,6]{1,0:T(1,128)S(1)}, s32[1,6]{1,0:T(1,128)}, u32[]{:S(2)}) copy-start(s32[1,6]{1,0:T(1,128)} %blocks_ref.1) | copy-start | bytes 76
  1.9 0.9 %copy-start = (f32[128,512]{1,0:T(8,128)S(1)}, f32[128,512]{1,0:T(8,128)}, u32[]{:S(2)}) copy-start(f32[128,512]{1,0:T(8,128)} %feat_ref.1) | copy-start | bytes 786436
  2.9 0.9 %copy-start.1 = (f32[128,512]{1,0:T(8,128)S(1)}, f32[128,512]{1,0:T(8,128)}, u32[]{:S(2)}) copy-start(f32[128,512]{1,0:T(8,128)} %cot_ref.1) | copy-start | bytes 786436
  3.8 0.8 %copy-start.2 = (s32[1,6,16,128]{3,2,1,0:T(8,128)S(1)}, s32[1,6,16,128]{3,2,1,0:T(8,128)}, u32[]{:S(2)}) copy-start(s32[1,6,16,128]{3,2,1,0:T(8,128)} %param.12) | copy-start | bytes 147460
  4.6 0.7 %copy-start.3 = (f32[8,64]{1,0:T(8,128)S(1)}, f32[8,64]{1,0:T(8,128)}, u32[]{:S(2)}) copy-start(f32[8,64]{1,0:T(8,128)} %source_ref.1) | copy-start | bytes 6148
  5.3 0.7 %copy-start.4 = (f32[8,64]{1,0:T(8,128)S(1)}, f32[8,64]{1,0:T(8,128)}, u32[]{:S(2)}) copy-start(f32[8,64]{1,0:T(8,128)} %target_ref.1) | copy-start | bytes 6148

commit v2 on v1

--- a/solution.py
+++ b/solution.py
@@ -25,17 +25,23 @@
 def kernel(
     cycle,
     copies,
-    feat_ref,
+    feat_hbm,
+    source_hbm,
+    target_hbm,
+    blocks_hbm,
+    live_hbm,
+    edges_hbm,
+    cot_hbm,
+    out_ref,
+    grad_ref,
+    sgrad_ref,
+    tgrad_ref,
     source_ref,
     target_ref,
     blocks_ref,
     live_ref,
     edges_ref,
     cot_ref,
-    out_ref,
-    grad_ref,
-    sgrad_ref,
-    tgrad_ref,
     feats,
     srcs,
     bits,
@@ -64,8 +70,15 @@
     red_recv,
     red2_send,
     red2_recv,
+    local_sem,
+    low_recv,
+    near_send,
+    far_send,
+    low_send,
 ):
-    rows, width = feat_ref.shape
+    rows, width = feat_hbm.shape
+    half = rows // 2
+    feat_ref = feats.at[0]
     heads, head = source_ref.shape
     slots = edges_ref.shape[0]
     count = 3 * copies
@@ -75,12 +88,29 @@
 
     def place(c):
         group, turn = c // copies, c % copies
-        shift = (group + 1) % 3 - 1
+        shift = ((group + 1) % 3 - 1) * (1 - 2 * lax.rem(blk, 2))
         return lax.rem(blk + shift + cycle, cycle), lax.rem(cp + turn, copies)
 
     def mirror(c):
         group, turn = c // copies, c % copies
-        return (3 - group) % 3 * copies + (copies - turn) % copies
+        return group * copies + (copies - turn) % copies
+
+    loads = [
+        pltpu.make_async_copy(source, target, local_sem.at[i])
+        for i, (source, target) in enumerate(
+            (
+                (feat_hbm, feat_ref),
+                (source_hbm, source_ref),
+                (target_hbm, target_ref),
+                (blocks_hbm, blocks_ref),
+                (live_hbm, live_ref),
+                (edges_hbm, edges_ref),
+                (cot_hbm, cot_ref),
+            )
+        )
+    ]
+    for load in loads:
+        load.start()
 
     barrier = pltpu.get_barrier_semaphore()
     for c in range(1, count):
@@ -94,6 +124,8 @@
 
     lax.fori_loop(2, cycle - 1, greet, 0)
 
+    for load in loads[:3]:
+        load.wait()
     lane = lax.broadcasted_iota(jnp.int32, (heads, width), 1)
     head_row = lax.broadcasted_iota(jnp.int32, (heads, width), 0)
     on_head = lane // head == head_row
@@ -123,11 +155,41 @@
 
     def feat_copy(c):
         return pltpu.make_async_remote_copy(
-            src_ref=feat_ref,
+            src_ref=feat_hbm,
             dst_ref=feats.at[mirror(c)],
             send_sem=feat_send.at[c],
             recv_sem=feat_recv.at[mirror(c)],
             device_id=place(c),
+            device_id_type=MESH,
+        )
+
+    def near_copy(turn):
+        return pltpu.make_async_remote_copy(
+            src_ref=feats.at[turn],
+            dst_ref=feats.at[copies + turn],
+            send_sem=near_send.at[turn],
+            recv_sem=feat_recv.at[copies + turn],
+            device_id=place(copies),
+            device_id_type=MESH,
+        )
+
+    def far_copy(turn):
+        return pltpu.make_async_remote_copy(
+            src_ref=feats.at[turn, pl.ds(0, half)],
+            dst_ref=feats.at[2 * copies + turn, pl.ds(0, half)],
+            send_sem=far_send.at[turn],
+            recv_sem=feat_recv.at[2 * copies + turn],
+            device_id=place(2 * copies),
+            device_id_type=MESH,
+        )
+
+    def low_copy(turn):
+        return pltpu.make_async_remote_copy(
+            src_ref=feats.at[2 * copies, pl.ds(half, half)],
+            dst_ref=feats.at[mirror(2 * copies + turn), pl.ds(half, half)],
+            send_sem=low_send.at[turn],
+            recv_sem=low_recv.at[mirror(turn)],
+            device_id=place(turn),
             device_id_type=MESH,
         )
 
@@ -143,17 +205,19 @@
 
     for c in range(1, count):
         src_copy(c).start()
-    for c in range(1, count):
+    direct = list(range(1, copies)) + [2 * copies, copies]
+    for c in direct:
         feat_copy(c).start()
-    feats[0] = feat_ref[...]
-
-    live = live_ref[0]
+    for load in loads[3:]:
+        load.wait()
+
+    live = live_ref[...]
     for c in range(count):
         there, turn = place(c)
         block = there * copies + turn
         words = jnp.zeros(bits.shape[1:], jnp.int32)
         for slot in range(slots):
-            chosen = jnp.logical_and(blocks_ref[0, slot] == block, slot < live)
+            chosen = jnp.logical_and(blocks_ref[:, slot : slot + 1] == block, slot < live)
             words = words + edges_ref[slot] * jnp.where(chosen, 1, 0)
         bits[c] = words
 
@@ -205,14 +269,31 @@
         return tuple(sums)
 
     zero_row = jnp.zeros((1, rows), f32)
-    norms = lax.fori_loop(0, count, weight_step, (zero_row,) * heads)
+    norms = lax.fori_loop(0, copies + 1, weight_step, (zero_row,) * heads)
+    for turn in range(1, copies):
+        feat_copy(mirror(turn)).wait_recv()
+        far_copy(turn).start()
+        near_copy(turn).start()
+    feat_copy(2 * copies).wait_recv()
+    for turn in range(1, copies):
+        low_copy(turn).start()
+    norms = lax.fori_loop(copies + 1, count, weight_step, norms)
 
     agg[...] = jnp.zeros(agg.shape, f32)
 
     def forward_step(c, carry):
-        @pl.when(c > 0)
+        @pl.when(c == copies)
         def _():
-            feat_copy(mirror(c)).wait_recv()
+            feat_copy(copies).wait_recv()
+
+        @pl.when(jnp.logical_and(c > copies, c < 2 * copies))
+        def _():
+            near_copy(c - copies).wait_recv()
+
+        @pl.when(c > 2 * copies)
+        def _():
+            far_copy(c - 2 * copies).wait_recv()
+            low_copy(mirror(c - 2 * copies)).wait_recv()
 
         high, low = split(feats[c].T)
         both = jnp.concatenate([high, low], 1)
@@ -373,8 +454,13 @@
 
     for c in range(1, count):
         src_copy(c).wait_send()
+        grad_copy(c).wait_send()
+    for c in direct:
         feat_copy(c).wait_send()
-        grad_copy(c).wait_send()
+    for turn in range(1, copies):
+        near_copy(turn).wait_send()
+        far_copy(turn).wait_send()
+        low_copy(turn).wait_send()
 
     def red_sent(step, carry):
         red_copy(step, blk).wait_send()
@@ -383,6 +469,18 @@
     lax.fori_loop(1, cycle, red_sent, 0)
     for turn in range(1, copies):
         red2_copy(turn, cp).wait_send()
+
+
+def settle(*refs):
+    sems = refs[-1]
+    count = len(refs) // 2
+    moves = [
+        pltpu.make_async_copy(refs[i], refs[count + i], sems.at[i]) for i in range(count)
+    ]
+    for move in moves:
+        move.start()
+    for move in moves:
+        move.wait()
 
 
 def per_device(
@@ -396,19 +494,27 @@
     pairs = heads // 2
     slots, word_rows = edge_bits.shape[1:3]
     vmem = pl.BlockSpec(memory_space=pltpu.VMEM)
-    smem = pl.BlockSpec(memory_space=pltpu.SMEM)
+    hbm = pl.BlockSpec(memory_space=pltpu.HBM)
+    anywhere = pl.BlockSpec(memory_space=pl.ANY)
     dma = pltpu.SemaphoreType.DMA
-    return pl.pallas_call(
+    shapes = (
+        jax.ShapeDtypeStruct((rows, width), f32),
+        jax.ShapeDtypeStruct((rows, width), f32),
+        jax.ShapeDtypeStruct((heads, head), f32),
+        jax.ShapeDtypeStruct((heads, head), f32),
+    )
+    found = pl.pallas_call(
         functools.partial(kernel, cycle, copies),
-        out_shape=(
-            jax.ShapeDtypeStruct((rows, width), f32),
-            jax.ShapeDtypeStruct((rows, width), f32),
-            jax.ShapeDtypeStruct((heads, head), f32),
-            jax.ShapeDtypeStruct((heads, head), f32),
-        ),
-        in_specs=[vmem, vmem, vmem, smem, smem, vmem, vmem],
+        out_shape=shapes,
+        in_specs=[hbm] * 7,
         out_specs=(vmem,) * 4,
         scratch_shapes=[
+            pltpu.VMEM((heads, head), f32),
+            pltpu.VMEM((heads, head), f32),
+            pltpu.VMEM((1, slots), jnp.int32),
+            pltpu.VMEM((1, 1), jnp.int32),
+            pltpu.VMEM((slots, word_rows, rows), jnp.int32),
+            pltpu.VMEM((rows, width), f32),
             pltpu.VMEM((count, rows, width), f32),
             pltpu.VMEM((count, heads, rows), f32),
             pltpu.VMEM((count, word_rows, rows), jnp.int32),
@@ -437,19 +543,32 @@
             dma((cycle,)),
             dma((copies,)),
             dma((copies,)),
+            dma((7,)),
+            dma((copies,)),
+            dma((copies,)),
+            dma((copies,)),
+            dma((copies,)),
         ],
         compiler_params=pltpu.CompilerParams(
-            collective_id=0, has_side_effects=True, vmem_limit_bytes=52 * 1024 * 1024
+            collective_id=0, has_side_effects=True, vmem_limit_bytes=63 * 1024 * 1024
         ),
     )(
         features,
         attend_source,
         attend_target,
         key_blocks,
-        live_slots,
+        live_slots.reshape(1, 1),
         edge_bits.reshape(slots, word_rows, rows),
         cotangent,
     )
+    return pl.pallas_call(
+        settle,
+        out_shape=shapes,
+        in_specs=[anywhere] * 4,
+        out_specs=(anywhere,) * 4,
+        scratch_shapes=[dma((4,))],
+        compiler_params=pltpu.CompilerParams(vmem_limit_bytes=63 * 1024 * 1024),
+    )(*found)
 
 
 def solution(mesh):

time: 57.5 us -> 59.4 us (1.033); the launches traced: 56.7 us -> 59.2 us
  Pallas kernels: 48.1 us -> 57.9 us
  local copies, waits for them, and re-layouts: 7.31 us -> 0 us
    pallas_call x1 -> x2, Pallas kernels: 48.1 us -> 57.9 us  [the longest x1 40.6 us: per_device(): pl.pallas_call(functools.partial(kernel, cycle, copies), out_shape=shapes...]
    unnamed x16 -> x0, local copies, waits for them, and re-layouts: 7.31 us -> none
where the time goes in v2:
time: 59.4 us; the launch traced here: 59.2 us
  Pallas kernels  57.9 us (97%)
  between operations  1.29 us (2%)
    pallas_call x1, Pallas kernels, per_device(): pl.pallas_call(functools.partial(kernel, cycle, copies), out_shape=shapes...  40.6 us
    pallas_call x1, Pallas kernels, per_device(): pl.pallas_call(settle, out_shape=shapes, in_specs=[anywhere] * 4, out_spe...  17.3 us

profile of v2, /device:TPU:1, one launch (start us, length us, event | category | flops | bytes accessed | tf_op | source)
XLA Modules:
  0.0 59.2 jit_solution(2986226333555802974)
XLA Ops:
  1.3 40.6 %shard_map.102 = (f32[128,512]{1,0:T(8,128)}, f32[128,512]{1,0:T(8,128)}, f32[8,64]{1,0:T(8,128)}, f32[8,64]{1,0:T(8,128)}) custom-call(f32[128,512]{1,0:T(8,128)} %feat_hbm.1, f32[8,64]{1,0:T(8,128)} %source_hbm.1, f32[8,64]{1,0:T(8,128)} %target_hbm.1, s32[1,6]{1,0:T(1,128)} %blocks_hbm.1, s32[1,1]{1,0:T(1,128)} %bitcast.2.live_hbm, ...), custom_call_target="tpu_custom_call" | custom-call | tf_op jit(solution)/shard_map/pallas_call | solution.py:506
  41.9 17.3 %shard_map.103 = (f32[128,512]{1,0:T(8,128)}, f32[128,512]{1,0:T(8,128)}, f32[8,64]{1,0:T(8,128)}, f32[8,64]{1,0:T(8,128)}) custom-call(f32[128,512]{1,0:T(8,128)} %get-tuple-element.8.refs_0_, f32[128,512]{1,0:T(8,128)} %get-tuple-element.9.refs_1_, f32[8,64]{1,0:T(8,128)} %get-tuple-element.10.refs_2_, f32[8,64]{1,0:T(8,128)} %get-tuple-element.11.refs_3_), custom_call_target="tpu_custom_call" | custom-call | tf_op jit(solution)/shard_map/pallas_call | solution.py:564

commit v3 on v2

--- a/solution.py
+++ b/solution.py
@@ -564,7 +564,7 @@
     return pl.pallas_call(
         settle,
         out_shape=shapes,
-        in_specs=[anywhere] * 4,
+        in_specs=[vmem] * 4,
         out_specs=(anywhere,) * 4,
         scratch_shapes=[dma((4,))],
         compiler_params=pltpu.CompilerParams(vmem_limit_bytes=63 * 1024 * 1024),

time: 59.4 us -> 44 us (0.74)
  Pallas kernels: 57.9 us -> 42.5 us
    pallas_call x1, Pallas kernels: 17.3 us -> 1.86 us  [per_device(): pl.pallas_call(settle, out_shape=shapes, in_specs=[vmem] * 4, out_specs=(...]
where the time goes in v3:
time: 44 us; the launch traced here: 43.8 us
  Pallas kernels  42.5 us (97%)
  between operations  1.29 us (3%)
    pallas_call x1, Pallas kernels, per_device(): pl.pallas_call(functools.partial(kernel, cycle, copies), out_shape=shapes...  40.6 us
    pallas_call x1, Pallas kernels, per_device(): pl.pallas_call(settle, out_shape=shapes, in_specs=[vmem] * 4, out_specs=(...  1.86 us

profile of v3, /device:TPU:1, one launch (start us, length us, event | category | flops | bytes accessed | tf_op | source)
XLA Modules:
  0.0 43.8 jit_solution(9271996718378348660)
XLA Ops:
  1.3 40.6 %shard_map.102 = (f32[128,512]{1,0:T(8,128)}, f32[128,512]{1,0:T(8,128)}, f32[8,64]{1,0:T(8,128)}, f32[8,64]{1,0:T(8,128)}) custom-call(f32[128,512]{1,0:T(8,128)} %feat_hbm.1, f32[8,64]{1,0:T(8,128)} %source_hbm.1, f32[8,64]{1,0:T(8,128)} %target_hbm.1, s32[1,6]{1,0:T(1,128)} %blocks_hbm.1, s32[1,1]{1,0:T(1,128)} %bitcast.2.live_hbm, ...), custom_call_target="tpu_custom_call" | custom-call | tf_op jit(solution)/shard_map/pallas_call | solution.py:506
  41.9 1.9 %shard_map.103 = (f32[128,512]{1,0:T(8,128)}, f32[128,512]{1,0:T(8,128)}, f32[8,64]{1,0:T(8,128)}, f32[8,64]{1,0:T(8,128)}) custom-call(f32[128,512]{1,0:T(8,128)} %get-tuple-element.8.refs_0_, f32[128,512]{1,0:T(8,128)} %get-tuple-element.9.refs_1_, f32[8,64]{1,0:T(8,128)} %get-tuple-element.10.refs_2_, f32[8,64]{1,0:T(8,128)} %get-tuple-element.11.refs_3_), custom_call_target="tpu_custom_call" | custom-call | tf_op jit(solution)/shard_map/pallas_call | solution.py:564

commit v4 on v3

--- a/solution.py
+++ b/solution.py
@@ -75,6 +75,8 @@
     near_send,
     far_send,
     low_send,
+    glow_send,
+    glow_recv,
 ):
     rows, width = feat_hbm.shape
     half = rows // 2
@@ -193,13 +195,53 @@
             device_id_type=MESH,
         )
 
-    def grad_copy(c):
-        return pltpu.make_async_remote_copy(
-            src_ref=sent.at[c],
-            dst_ref=got.at[mirror(c)],
-            send_sem=grad_send.at[c],
-            recv_sem=grad_recv.at[mirror(c)],
-            device_id=place(c),
+    def own_grad(turn):
+        return pltpu.make_async_remote_copy(
+            src_ref=sent.at[turn],
+            dst_ref=got.at[mirror(turn)],
+            send_sem=grad_send.at[turn],
+            recv_sem=grad_recv.at[mirror(turn)],
+            device_id=place(turn),
+            device_id_type=MESH,
+        )
+
+    def near_grad(turn):
+        return pltpu.make_async_remote_copy(
+            src_ref=sent.at[copies + turn],
+            dst_ref=got.at[copies + turn],
+            send_sem=grad_send.at[copies + turn],
+            recv_sem=grad_recv.at[copies + turn],
+            device_id=place(copies),
+            device_id_type=MESH,
+        )
+
+    def far_grad(turn):
+        return pltpu.make_async_remote_copy(
+            src_ref=sent.at[2 * copies + turn, pl.ds(0, half)],
+            dst_ref=got.at[2 * copies + turn, pl.ds(0, half)],
+            send_sem=grad_send.at[2 * copies + turn],
+            recv_sem=grad_recv.at[2 * copies + turn],
+            device_id=place(2 * copies),
+            device_id_type=MESH,
+        )
+
+    def low_grad(turn):
+        return pltpu.make_async_remote_copy(
+            src_ref=sent.at[2 * copies + turn, pl.ds(half, half)],
+            dst_ref=got.at[2 * copies + mirror(turn), pl.ds(half, half)],
+            send_sem=glow_send.at[turn],
+            recv_sem=glow_recv.at[mirror(turn)],
+            device_id=place(turn),
+            device_id_type=MESH,
+        )
+
+    def low_sum():
+        return pltpu.make_async_remote_copy(
+            src_ref=sent.at[2 * copies, pl.ds(half, half)],
+            dst_ref=got.at[2 * copies, pl.ds(half, half)],
+            send_sem=glow_send.at[0],
+            recv_sem=glow_recv.at[0],
+            device_id=place(2 * copies),
             device_id_type=MESH,
         )
 
@@ -355,8 +397,7 @@
     dst_sum[...] = jnp.zeros(dst_sum.shape, f32)
     src_att[...] = jnp.zeros(src_att.shape, f32)
 
-    def backward_step(step, carry):
-        c = lax.rem(step + 1, count)
+    def backward(c):
         for p in range(pairs):
             tile = pl.ds(p * 2 * head, 2 * head)
             value = feats[c, :, tile]
@@ -376,13 +417,40 @@
             sent[c, :, tile] = both[:, : 2 * head]
             src_att[p] += jnp.sum(both[:, 2 * head :] * value, axis=0, keepdims=True)
 
-        @pl.when(c > 0)
-        def _():
-            grad_copy(c).start()
-
-        return carry
-
-    lax.fori_loop(0, count, backward_step, 0)
+    def far_step(turn, carry):
+        backward(2 * copies + turn)
+        low_grad(turn).start()
+        far_grad(turn).start()
+        return carry
+
+    lax.fori_loop(1, copies, far_step, 0)
+
+    def near_step(turn, carry):
+        backward(copies + turn)
+        near_grad(turn).start()
+        return carry
+
+    lax.fori_loop(1, copies, near_step, 0)
+    backward(2 * copies)
+    far_grad(0).start()
+
+    def own_step(turn, carry):
+        backward(turn)
+        near_grad(turn).wait_recv()
+        far_grad(turn).wait_recv()
+        sent[turn] += got[copies + turn]
+        sent[turn, :half] += got[2 * copies + turn, :half]
+        own_grad(turn).start()
+        return carry
+
+    lax.fori_loop(1, copies, own_step, 0)
+    for turn in range(1, copies):
+        low_grad(mirror(turn)).wait_recv()
+        sent[2 * copies, half:] += got[2 * copies + turn, half:]
+    low_sum().start()
+    backward(copies)
+    near_grad(0).start()
+    backward(0)
 
     dst_rows = jnp.concatenate([dst_sum[h] for h in range(heads)], 0)
     tgt_att = jnp.dot(dst_rows, feat_ref[...], precision=precise, preferred_element_type=f32)
@@ -433,12 +501,13 @@
     for turn in range(1, copies):
         red2_copy(turn, cp).start()
 
-    def grad_step(c, carry):
-        grad_copy(mirror(c)).wait_recv()
-        grad_ref[...] += got[c]
-        return carry
-
-    lax.fori_loop(1, count, grad_step, 0)
+    near_grad(0).wait_recv()
+    far_grad(0).wait_recv()
+    low_sum().wait_recv()
+    grad_ref[...] += got[copies] + got[2 * copies]
+    for turn in range(1, copies):
+        own_grad(mirror(turn)).wait_recv()
+        grad_ref[...] += got[turn]
 
     for turn in range(1, copies):
         red2_copy(turn, lax.rem(cp + turn, copies)).wait_recv()
@@ -454,13 +523,18 @@
 
     for c in range(1, count):
         src_copy(c).wait_send()
-        grad_copy(c).wait_send()
     for c in direct:
         feat_copy(c).wait_send()
     for turn in range(1, copies):
         near_copy(turn).wait_send()
         far_copy(turn).wait_send()
         low_copy(turn).wait_send()
+        own_grad(turn).wait_send()
+        low_grad(turn).wait_send()
+    for turn in range(copies):
+        near_grad(turn).wait_send()
+        far_grad(turn).wait_send()
+    low_sum().wait_send()
 
     def red_sent(step, carry):
         red_copy(step, blk).wait_send()
@@ -548,6 +622,8 @@
             dma((copies,)),
             dma((copies,)),
             dma((copies,)),
+            dma((copies,)),
+            dma((copies,)),
         ],
         compiler_params=pltpu.CompilerParams(
             collective_id=0, has_side_effects=True, vmem_limit_bytes=63 * 1024 * 1024

time: 44 us -> 40 us (0.909)
  the two profiles are of different devices: /device:TPU:1 before, /device:TPU:0 now
where the time goes in v4:
time: 40 us; the launch traced here: 39.9 us
  Pallas kernels  38.6 us (96%)
  between operations  1.29 us (3%)
    pallas_call x1, Pallas kernels, per_device(): pl.pallas_call(functools.partial(kernel, cycle, copies), out_shape=shapes...  36.7 us
    pallas_call x1, Pallas kernels, per_device(): pl.pallas_call(settle, out_shape=shapes, in_specs=[vmem] * 4, out_specs=(...  1.86 us

profile of v4, /device:TPU:0, one launch (start us, length us, event | category | flops | bytes accessed | tf_op | source)
XLA Modules:
  0.0 39.9 jit_solution(13571452474321916881)
XLA Ops:
  1.3 36.7 %shard_map.102 = (f32[128,512]{1,0:T(8,128)}, f32[128,512]{1,0:T(8,128)}, f32[8,64]{1,0:T(8,128)}, f32[8,64]{1,0:T(8,128)}) custom-call(f32[128,512]{1,0:T(8,128)} %feat_hbm.1, f32[8,64]{1,0:T(8,128)} %source_hbm.1, f32[8,64]{1,0:T(8,128)} %target_hbm.1, s32[1,6]{1,0:T(1,128)} %blocks_hbm.1, s32[1,1]{1,0:T(1,128)} %bitcast.2.live_hbm, ...), custom_call_target="tpu_custom_call" | custom-call | tf_op jit(solution)/shard_map/pallas_call | solution.py:580
  38.0 1.9 %shard_map.103 = (f32[128,512]{1,0:T(8,128)}, f32[128,512]{1,0:T(8,128)}, f32[8,64]{1,0:T(8,128)}, f32[8,64]{1,0:T(8,128)}) custom-call(f32[128,512]{1,0:T(8,128)} %get-tuple-element.8.refs_0_, f32[128,512]{1,0:T(8,128)} %get-tuple-element.9.refs_1_, f32[8,64]{1,0:T(8,128)} %get-tuple-element.10.refs_2_, f32[8,64]{1,0:T(8,128)} %get-tuple-element.11.refs_3_), custom_call_target="tpu_custom_call" | custom-call | tf_op jit(solution)/shard_map/pallas_call | solution.py:640
